TPU v7x, 512 devices: a whole 4x8x8 slice. The times are simulated.
512 devices in a mesh: dp: 64 (over z, y), tensor: 8 (over x, core).
Axes of the slice: x: 4, y: 8, z: 8, core: 2. Of those that a mesh axis runs over, the one named last changes fastest.
Arguments:
- queries: bfloat16 [4096, 8, 8192], P('dp', None, 'tensor'), may hold values from -150 to 150
- text_kv: bfloat16 [4096, 8, 2048], P('dp', None, 'tensor'), may hold values from -7 to 7
- visual_kv: bfloat16 [256, 64, 2048], P('dp', None, 'tensor'), may hold values from -6 to 6
- loss_gain: float32 [8192], P('tensor'), may hold values from 0.5 to 4.5
- response_image: int32 [4096], replicated, may hold values from 0 to 255, as said below
- visual_rows: int32 [256], replicated, may hold values from 1 to 64, as said below
- text_length: int32 [4096], replicated, may hold values from 1 to 8, as said below
Outputs:
- visual_grad: bfloat16 [256, 64, 2048], P('dp', None, 'tensor')
- text_grad: bfloat16 [4096, 8, 2048], P('dp', None, 'tensor')
- loss: float32 [4096], P('dp')
Inputs may be any that keep to these rules, and one draw needn't show every extreme that they name: For each d, the responses d * 64 to d * 64 + 63 have images of every index of dp once each: response_image[r] // 4 takes each value 0 to 63 once among them. Every image has exactly 16 responses. `visual_rows`: some image uses all 64 rows. `text_length`: some response uses all 8 tokens.
All inputs are finite; a program needn't handle non-finite values.
Results may differ from a plain program's by a relative error of at most 0.04.
Values may be sent and summed in bfloat16 or wider, within the bound.
A program may use at most 64 MiB of HBM per device.

v0:
```python
import jax
import jax.numpy as jnp
from jax import lax
from jax.sharding import PartitionSpec as P

HD = 128


def multiply(form, left, right):
    return jnp.einsum(form, left, right, preferred_element_type=jnp.float32)


def attend(queries, text_kv, image_kv, seen_rows, length, loss_gain):
    resp_count, text_steps, query_width = queries.shape
    kv_heads = text_kv.shape[-1] // (2 * HD)
    groups = query_width // (HD * kv_heads)
    vis_rows = image_kv.shape[1]
    all_rows = vis_rows + text_steps
    query_heads = queries.reshape(resp_count, text_steps, kv_heads, groups, HD)
    key_value = jnp.concatenate([image_kv, text_kv], axis=1).reshape(
        resp_count, all_rows, kv_heads, 2, HD
    )
    key_rows = key_value[:, :, :, 0]
    value_rows = key_value[:, :, :, 1]
    scores = multiply("jtkgd,jskd->jkgts", query_heads, key_rows) * HD ** (-0.5)
    key_index = jnp.arange(all_rows, dtype=jnp.int32)
    query_index = jnp.arange(text_steps, dtype=jnp.int32)
    vis_allowed = key_index[None, None, :] < seen_rows[:, None, None]
    text_index = key_index - vis_rows
    text_allowed = (
        (key_index[None, None, :] >= vis_rows)
        & (text_index[None, None, :] <= query_index[None, :, None])
        & (text_index[None, None, :] < length[:, None, None])
    )
    allowed = vis_allowed | text_allowed
    scores = jnp.where(allowed[:, None, None], scores, jnp.float32(-1e30))
    row_max = jnp.max(scores, axis=-1, keepdims=True)
    raw_weights = jnp.exp(scores - row_max)
    prob = raw_weights / jnp.sum(raw_weights, axis=-1, keepdims=True)
    prob_bf = prob.astype(jnp.bfloat16)
    attended = multiply("jkgts,jskd->jtkgd", prob_bf, value_rows)
    flat_out = attended.reshape(resp_count, text_steps, query_width)
    live_mask = (query_index[None, :] < length[:, None]).astype(jnp.float32)
    loss_part = jnp.sum(
        live_mask[:, :, None] * loss_gain[None, None, :] * flat_out * flat_out, axis=(1, 2)
    ) / (2.0 * text_steps * HD)
    cotangent = (live_mask[:, :, None] * loss_gain[None, None, :] * flat_out).astype(jnp.bfloat16)
    cot_heads = cotangent.reshape(resp_count, text_steps, kv_heads, groups, HD)
    value_grad = multiply("jkgts,jtkgd->jskd", prob_bf, cot_heads)
    prob_grad = multiply("jtkgd,jskd->jkgts", cot_heads, value_rows)
    row_delta = jnp.transpose(
        jnp.sum(cot_heads.astype(jnp.float32) * attended, axis=-1), (0, 2, 3, 1)
    )
    score_grad = (prob * (prob_grad - row_delta[..., None])).astype(jnp.bfloat16)
    key_grad = multiply("jkgts,jtkgd->jskd", score_grad, query_heads) * HD ** (-0.5)
    all_grads = jnp.stack([key_grad, value_grad], axis=3).reshape(
        resp_count, all_rows, 2 * kv_heads * HD
    )
    return (loss_part, all_grads[:, :vis_rows], all_grads[:, vis_rows:])


def lookup(counts_table, wanted):
    matches = wanted[:, None] == jnp.arange(counts_table.shape[0], dtype=jnp.int32)[None, :]
    return jnp.sum(jnp.where(matches, counts_table[None, :], 0), axis=1)


def local(queries, text_kv, visual_kv, loss_gain, response_image, visual_rows, text_length):
    dp_count = lax.axis_size("dp")
    place = lax.axis_index("dp")
    owned = visual_kv.shape[0]
    image_table = response_image.reshape(dp_count, dp_count)
    span_table = text_length.reshape(dp_count, dp_count)
    positions = jnp.arange(dp_count, dtype=jnp.int32)
    my_images = lax.dynamic_index_in_dim(image_table, place, 0, keepdims=False)
    my_spans = lax.dynamic_index_in_dim(span_table, place, 0, keepdims=False)
    owner_row = my_images // owned
    slot_of_owner = jnp.sum(
        jnp.where(owner_row[None, :] == positions[:, None], positions[None, :], 0), axis=1
    )
    mine_all = image_table // owned == place
    column = jnp.sum(jnp.where(mine_all, image_table, 0), axis=1)
    local_slot = column - place * owned
    selector = (local_slot[:, None] == jnp.arange(owned, dtype=jnp.int32)[None, :]).astype(
        jnp.bfloat16
    )
    outgoing = jnp.take(visual_kv, local_slot, axis=0)
    arrived = lax.all_to_all(outgoing, "dp", split_axis=0, concat_axis=0, tiled=True)
    slot_rows = jnp.take(arrived, owner_row, axis=0)
    partial_loss, vis_grad, txt_grad = attend(
        queries, text_kv, slot_rows, lookup(visual_rows, my_images), my_spans, loss_gain
    )
    by_owner = jnp.take(vis_grad.astype(jnp.bfloat16), slot_of_owner, axis=0)
    returned = lax.all_to_all(by_owner, "dp", split_axis=0, concat_axis=0, tiled=True)
    text_grad = txt_grad.astype(jnp.bfloat16)
    visual_grad = jnp.einsum(
        "dvc,dk->kvc", returned, selector, preferred_element_type=jnp.float32
    ).astype(jnp.bfloat16)
    loss = lax.psum(partial_loss, "tensor")
    return (visual_grad, text_grad, loss)


def solution(mesh):
    in_specs = (
        P("dp", None, "tensor"),
        P("dp", None, "tensor"),
        P("dp", None, "tensor"),
        P("tensor"),
        P(),
        P(),
        P(),
    )
    out_specs = (P("dp", None, "tensor"), P("dp", None, "tensor"), P("dp"))
    return jax.shard_map(local, mesh=mesh, in_specs=in_specs, out_specs=out_specs, check_vma=False)
```

profile of v0, /device:TPU:4, one launch (start us, length us, event | category | flops | bytes accessed | tf_op | source)
XLA Modules:
  0.0 188.3 jit_solution(8047185058686727100)
XLA Ops:
  1.8 1.6 gather_fusion
  3.4 1.6 broadcast_select_fusion.2
  5.0 16.7 %all-to-all-start = ((bf16[64,64,256]{2,1,0:T(8,128)(2,1)}), bf16[64,64,256]{2,1,0:T(8,128)(2,1)S(1)}, u32[]{:S(2)}, u32[]{:S(2)}) async-start(bf16[64,64,256]{2,1,0:T(8,128)(2,1)} %broadcast_select_fusion.2), calls=%async_computation | async-start | bytes 4194304 | tf_op jit(solution)/shard_map/all_to_all | solution.py:87
  22.4 51.8 %all-to-all-done = bf16[64,64,256]{2,1,0:T(8,128)(2,1)S(1)} async-done(((bf16[64,64,256]{2,1,0:T(8,128)(2,1)}), bf16[64,64,256]{2,1,0:T(8,128)(2,1)S(1)}, u32[]{:S(2)}, u32[]{:S(2)}) %all-to-all-start) | async-done | bytes 2097184 | tf_op jit(solution)/shard_map/all_to_all | solution.py:87
  74.1 2.0 %gather_fusion.1 = bf16[64,64,256]{2,1,0:T(8,128)(2,1)} fusion(bf16[64,64,256]{2,1,0:T(8,128)(2,1)S(1)} %all-to-all-done, s32[1024]{0:T(1024)S(1)} %pad_clamp_fusion.1), kind=kCustom, calls=%fused_computation.clone | custom fusion | bytes 4194560 | tf_op jit(solution)/shard_map/jit(_take)/gather | solution.py:88
  76.2 1.9 %broadcast_select_fusion.1 = bf16[64,64,256]{2,1,0:T(8,128)(2,1)S(1)} fusion(bf16[64,64,256]{2,1,0:T(8,128)(2,1)} %gather_fusion.1, pred[64]{0:T(512)(128)(4,1)S(1)} %get-tuple-element.18), kind=kLoop, calls=%fused_computation.21 | loop fusion | flops 1048576 | bytes 4194368 | tf_op jit(solution)/shard_map/jit(_take)/select_n | solution.py:88
  78.1 1.6 pad_maximum_fusion
  79.7 4.6 %reshape.252 = bf16[64,72,1,2,128]{4,3,1,0,2:T(2,128)(2,1)S(1)} reshape(bf16[64,72,256]{2,1,0:T(8,128)(2,1)} %pad_maximum_fusion) | data formatting | bytes 4718592 | tf_op jit(solution)/shard_map/reshape | solution.py:20
  84.3 3.3 %fusion.36 = (bf16[64,72,1,1,128]{4,3,1,0,2:T(2,128)(2,1)S(1)}, bf16[64,72,1,1,128]{4,3,1,0,2:T(2,128)(2,1)S(1)}) fusion(bf16[64,72,1,2,128]{4,3,1,0,2:T(2,128)(2,1)S(1)} %reshape.252), kind=kLoop, calls=%fused_computation.88 | loop fusion | bytes 4718592 | tf_op jit(solution)/shard_map/slice | solution.py:24
  88.5 1.3 fusion.9
  91.8 2.6 %fusion.4 = (f32[64]{0:T(128)S(1)}, f32[64,8,8]{1,2,0:T(8,128)}, bf16[64,8,8,128]{3,1,2,0:T(8,128)(2,1)}) fusion(f32[8,128]{1,0:T(8,128)S(1)} %bitcast.110, f32[64,8]{1,0:T(8,128)S(1)} %fusion.27, bf16[64,8,8,72]{3,1,2,0:T(8,128)(2,1)S(1)} %convert_bitcast_fusion, bf16[64,72,1,1,128]{4,3,1,0,2:T(2,128)(2,1)S(1)} %get-tuple-element.23), kind=kOutput, calls=%fused_computation.15 | convolution fusion | flops 79687616 | bytes 2840832 | tf_op jit(solution)/shard_map/jkgts,jskd->jtkgd/dot_general | solution.py:10
  94.4 1.8 copy.42
  96.2 3.4 %convolution_bitcast_fusion = bf16[64,72,1,1,128]{4,1,0,3,2:T(8,128)(2,1)} fusion(bf16[64,8,8,128]{3,1,2,0:T(8,128)(2,1)} %get-tuple-element.25, bf16[64,8,8,72]{3,1,2,0:T(8,128)(2,1)} %copy-done.1), kind=kOutput, calls=%fused_computation.25 | convolution fusion | flops 75497472 | bytes 2818048 | tf_op jit(solution)/shard_map/jkgts,jtkgd->jskd/dot_general | solution.py:10
  99.6 5.0 %fusion = bf16[64,72,1,1,128]{4,1,0,3,2:T(8,128)(2,1)} fusion(bf16[64,8,8,128]{3,1,2,0:T(8,128)(2,1)} %get-tuple-element.25, f32[64,8,8]{1,2,0:T(8,128)} %copy.42, bf16[64,8,8,128]{3,1,2,0:T(8,128)(2,1)S(1)} %bitcast.108, bf16[64,72,1,1,128]{4,3,1,0,2:T(2,128)(2,1)} %copy-done.2, f32[64,1,8,8,72]{4,2,3,0,1:T(8,128)S(1)} %get-tuple-element.27, ...), kind=kOutput, calls=%fused_computation.6 | convolution fusion | flops 153649152 | bytes 5685248 | tf_op jit(solution)/shard_map/jkgts,jtkgd->jskd/dot_general | solution.py:10
  104.6 1.8 maximum_convert_fusion
  106.5 3.8 %copy.45 = bf16[64,72,1,2,128]{4,3,1,0,2:T(2,128)(2,1)} copy(bf16[64,72,1,2,128]{4,1,0,3,2:T(8,128)(2,1)S(1)} %maximum_convert_fusion) | data formatting | bytes 4718592 | tf_op jit(solution)/shard_map/convert.1
  110.3 5.3 %reshape.260 = bf16[64,72,256]{2,1,0:T(8,128)(2,1)S(1)} reshape(bf16[64,72,1,2,128]{4,3,1,0,2:T(2,128)(2,1)} %copy.45) | data formatting | bytes 4718592 | tf_op jit(solution)/shard_map/convert.1
  115.6 1.6 slice.26
  117.3 3.6 %gather_fusion.2 = bf16[64,64,256]{2,1,0:T(8,128)(2,1)} fusion(bf16[64,64,256]{2,1,0:T(8,128)(2,1)} %slice.26, s32[1024]{0:T(1024)S(1)} %pad_clamp_fusion), kind=kCustom, calls=%fused_computation.1.clone | custom fusion | bytes 4194560 | tf_op jit(solution)/shard_map/jit(_take)/gather | solution.py:92
  120.8 3.1 %broadcast_select_fusion = bf16[64,64,256]{2,1,0:T(8,128)(2,1)} fusion(bf16[64,64,256]{2,1,0:T(8,128)(2,1)} %gather_fusion.2, pred[64]{0:T(512)(128)(4,1)S(1)} %get-tuple-element.28), kind=kLoop, calls=%fused_computation.20 | loop fusion | flops 1048576 | bytes 4194368 | tf_op jit(solution)/shard_map/jit(_take)/select_n | solution.py:92
  124.0 9.4 %all-to-all-start.1 = ((bf16[64,64,256]{2,1,0:T(8,128)(2,1)}), bf16[64,64,256]{2,1,0:T(8,128)(2,1)}, u32[]{:S(2)}, u32[]{:S(2)}) async-start(bf16[64,64,256]{2,1,0:T(8,128)(2,1)} %broadcast_select_fusion), calls=%async_computation.1 | async-start | bytes 4194304 | tf_op jit(solution)/shard_map/all_to_all | solution.py:93
  134.1 11.1 %psum.7 = f32[64]{0:T(128)} all-reduce(f32[64]{0:T(128)S(1)} %broadcast_multiply_fusion), channel_id=1, replica_groups=mesh['dp'=64,'tensor'=8] {'tensor'}, use_global_device_ids=true, to_apply=%region_7.9 | all-reduce | flops 64 | bytes 512 | tf_op jit(solution)/shard_map/psum | solution.py:98
  145.2 39.6 %all-to-all-done.1 = bf16[64,64,256]{2,1,0:T(8,128)(2,1)} async-done(((bf16[64,64,256]{2,1,0:T(8,128)(2,1)}), bf16[64,64,256]{2,1,0:T(8,128)(2,1)}, u32[]{:S(2)}, u32[]{:S(2)}) %all-to-all-start.1) | async-done | bytes 2097184 | tf_op jit(solution)/shard_map/all_to_all | solution.py:93
  184.8 2.8 %fusion.12 = bf16[4,64,256]{2,0,1:T(4,128)(2,1)S(1)} fusion(bf16[64,64,256]{2,1,0:T(8,128)(2,1)} %all-to-all-done.1, s32[64]{0:T(128)S(1)} %get-tuple-element.22), kind=kOutput, calls=%fused_computation.30 | convolution fusion | flops 8454400 | bytes 2228480 | tf_op jit(solution)/shard_map/dvc,dk->kvc/dot_general | solution.py:95
  (41 shorter events, 5.9 us)
Async XLA Ops:
  0.6 87.0 %copy-start = (bf16[64,8,1024]{2,1,0:T(8,128)(2,1)S(1)}, bf16[64,8,1024]{2,1,0:T(8,128)(2,1)}, u32[]{:S(2)}) copy-start(bf16[64,8,1024]{2,1,0:T(8,128)(2,1)} %param.9) | copy-start | bytes 3145732
  5.0 16.7 %copy-start.5 = (s32[4096]{0:T(1024)S(1)}, s32[4096]{0:T(1024)}, u32[]{:S(2)}) copy-start(s32[4096]{0:T(1024)} %param.15) | copy-start | bytes 49156
  5.0 16.9 %copy-start.6 = (s32[256]{0:T(256)S(1)}, s32[256]{0:T(256)}, u32[]{:S(2)}) copy-start(s32[256]{0:T(256)} %param.14) | copy-start | bytes 3076
  5.0 69.1 %all-to-all-start = ((bf16[64,64,256]{2,1,0:T(8,128)(2,1)}), bf16[64,64,256]{2,1,0:T(8,128)(2,1)S(1)}, u32[]{:S(2)}, u32[]{:S(2)}) async-start(bf16[64,64,256]{2,1,0:T(8,128)(2,1)} %broadcast_select_fusion.2), calls=%async_computation | async-start | bytes 4194304 | tf_op jit(solution)/shard_map/all_to_all | solution.py:87
  76.2 1.9 %copy-start.4 = (bf16[64,8,256]{2,1,0:T(8,128)(2,1)S(1)}, bf16[64,8,256]{2,1,0:T(8,128)(2,1)}, u32[]{:S(2)}) copy-start(bf16[64,8,256]{2,1,0:T(8,128)(2,1)} %param.10) | copy-start | bytes 786436
  87.6 4.2 %copy-start.2 = (bf16[64,72,1,1,128]{4,3,1,0,2:T(2,128)(2,1)}, bf16[64,72,1,1,128]{4,3,1,0,2:T(2,128)(2,1)S(1)}, u32[]{:S(2)}) copy-start(bf16[64,72,1,1,128]{4,3,1,0,2:T(2,128)(2,1)S(1)} %get-tuple-element.23) | copy-start | bytes 3538948
  89.8 0.7 copy-start.3
  90.5 1.3 copy-start.7
  91.8 2.6 %copy-start.1 = (bf16[64,8,8,72]{3,1,2,0:T(8,128)(2,1)}, bf16[64,8,8,72]{3,1,2,0:T(8,128)(2,1)S(1)}, u32[]{:S(2)}) copy-start(bf16[64,8,8,72]{3,1,2,0:T(8,128)(2,1)S(1)} %convert_bitcast_fusion) | copy-start | bytes 1769476
  124.0 60.8 %all-to-all-start.1 = ((bf16[64,64,256]{2,1,0:T(8,128)(2,1)}), bf16[64,64,256]{2,1,0:T(8,128)(2,1)}, u32[]{:S(2)}, u32[]{:S(2)}) async-start(bf16[64,64,256]{2,1,0:T(8,128)(2,1)} %broadcast_select_fusion), calls=%async_computation.1 | async-start | bytes 4194304 | tf_op jit(solution)/shard_map/all_to_all | solution.py:93
where the time goes:
time: 189 us; the launch traced here: 188 us
  waiting for transfers between devices  91.3 us (48%)
  local copies, waits for them, and re-layouts  30.8 us (16%)
  starting transfers between devices  26.1 us (14%)
  matrix products  14.7 us (8%)
  other arithmetic  13.4 us (7%)
  blocking collectives  11.1 us (6%)
    all_to_all x1, waiting for transfers between devices, local(): lax.all_to_all(outgoing, 'dp', split_axis=0, concat_axis=0, tiled=True)  51.8 us
    all_to_all x1, waiting for transfers between devices, local(): lax.all_to_all(by_owner, 'dp', split_axis=0, concat_axis=0, tiled=True)  39.6 us
    all_to_all x1, starting transfers between devices, local(): lax.all_to_all(outgoing, 'dp', split_axis=0, concat_axis=0, tiled=True)  16.7 us
    dot_general x4, matrix products, multiply(): return jnp.einsum(form, left, right, preferred_element_type=jnp.float32)  11.9 us
    psum x1, blocking collectives, local(): loss = lax.psum(partial_loss, 'tensor')  11.1 us
    all_to_all x1, starting transfers between devices, local(): lax.all_to_all(by_owner, 'dp', split_axis=0, concat_axis=0, tiled=True)  9.36 us
    another operation x2, local copies, waits for them, and re-layouts  9.18 us
    reshape x1, local copies, waits for them, and re-layouts, attend(): jnp.concatenate([image_kv, text_kv], axis=1)  4.63 us
  transfers between devices with their start and end apart: 2, of which 2 were waited for; matrix products, arithmetic and copies ran while one was open for 1% of the time, Pallas kernels for 0%

commit v1 on v0

v1 whole, which is shorter than its diff:
```python
import functools

import jax
import jax.numpy as jnp
from jax import lax
from jax.experimental import pallas as pl
from jax.experimental.pallas import tpu as pltpu
from jax.sharding import PartitionSpec as P

HD = 128
MESH = pl.DeviceIdType.MESH
SIDE = 8
N_DP = 64
TENSOR = 8
VIS = 64
TXT = 8
HEADS = 8
ROWS = HEADS * TXT
BLOCK = ROWS + 2 * TXT
KEYS = VIS + 2 * TXT
CHUNK = 8
SLOTS = N_DP
SCALE = HD ** (-0.5)

NT = (((1,), (1,)), ((), ()))
NN = (((1,), (0,)), ((), ()))
TN = (((0,), (0,)), ((), ()))


def dot(left, right, dims):
    return lax.dot_general(left, right, dims, preferred_element_type=jnp.float32)


def offset(group, turn):
    a, b = 1 + group % 4, 3 - group // 4
    last = group // 15
    if turn == 0:
        return a, b
    if turn == 1:
        return b, -a
    if turn == 2:
        return -a, -b + 4 * last
    return -b, a - 4 * last


def kernel(
    meta, rows4, q_ref, text_ref, kv_ref, gain_ref, place_ref,
    vis_out, text_out, loss_out,
    send_buf, recv_buf, key4, val4, acc, back_send, back_recv, loss_send, loss_recv, loss_parts,
    send_sem, recv_sem, back_send_sem, back_recv_sem, loss_send_sem, loss_recv_sem, part_send_sem, part_recv_sem,
):
    me = lax.axis_index("dp")
    core = lax.axis_index("tensor")
    z, y = me // SIDE, me % SIDE

    def target(group, turn):
        dz, dy = offset(group, turn)
        return ((z + dz + SIDE) % SIDE) * SIDE + (y + dy + SIDE) % SIDE

    def origin(group, turn):
        dz, dy = offset(group, turn)
        return ((z - dz + SIDE) % SIDE) * SIDE + (y - dy + SIDE) % SIDE

    barrier = pltpu.get_barrier_semaphore()

    def greet(step, carry):
        peer = (me + step) % N_DP
        pl.semaphore_signal(barrier, inc=1, device_id=(peer, core), device_id_type=MESH)
        return carry

    lax.fori_loop(1, N_DP, greet, 0)
    for step in range(1, TENSOR):
        pl.semaphore_signal(barrier, inc=1, device_id=(me, (core + step) % TENSOR), device_id_type=MESH)

    for image in range(4):
        key4[image] = kv_ref[image, :, 0:HD]
        val4[image] = kv_ref[image, :, HD : 2 * HD]
    acc[...] = jnp.zeros_like(acc)
    pl.semaphore_wait(barrier, N_DP - 1 + TENSOR - 1)

    def stage(slot, peer, where):
        response = meta[0, peer]
        wide = q_ref[response].astype(jnp.float32)
        stacked = jnp.concatenate([wide[:, h * HD : (h + 1) * HD] for h in range(HEADS)], axis=0)
        where[slot, 0:ROWS] = stacked.astype(jnp.bfloat16)
        text = text_ref[response].astype(jnp.float32)
        pair = jnp.concatenate([text[:, 0:HD], text[:, HD : 2 * HD]], axis=0)
        where[slot, ROWS:BLOCK] = pair.astype(jnp.bfloat16)

    def send(slot, peer):
        pltpu.make_async_remote_copy(
            src_ref=send_buf.at[slot],
            dst_ref=recv_buf.at[slot],
            send_sem=send_sem.at[slot // CHUNK],
            recv_sem=recv_sem.at[slot // CHUNK],
            device_id=(peer, core),
            device_id_type=MESH,
        ).start()

    def dispatch(group, carry):
        for turn in range(4):
            slot, peer = 4 * group + turn, target(group, turn)
            stage(slot, peer, send_buf)
            send(slot, peer)
        return carry

    lax.fori_loop(0, 15, dispatch, 0)
    for turn in range(3):
        stage(60 + turn, target(15, turn), send_buf)
        send(60 + turn, target(15, turn))
    stage(63, me, recv_buf)

    lane = lax.broadcasted_iota(jnp.int32, (1, HD), 1)
    first = lane < ROWS
    step_of = lane % TXT
    row = lax.broadcasted_iota(jnp.int32, (VIS + TXT, HD), 0)
    gain_t = gain_ref[...]

    def key_rows(both):
        return jnp.where(first, both[0 : VIS + TXT], both[KEYS : KEYS + VIS + TXT])

    def value_rows(both):
        both = [jnp.concatenate([both[b : b + VIS], both[b + VIS + TXT : b + KEYS]], axis=0) for b in (0, KEYS)]
        return jnp.where(first, both[0], both[1])

    none = jnp.zeros((TXT, HD), jnp.float32)

    def diagonal(parts):
        values = jnp.concatenate(parts, axis=0)
        zero = jnp.zeros_like(values)
        return jnp.concatenate([jnp.where(first, values, zero), jnp.where(first, zero, values)], axis=0).astype(
            jnp.bfloat16
        )

    def work(slot, peers):
        images = [meta[1, peer] for peer in peers]
        lengths = [meta[2, peer] for peer in peers]
        seen = [rows4[image] for image in images]
        blocks = [recv_buf[slot + i] for i in range(2)]
        texts = [block[ROWS:BLOCK] for block in blocks]
        queries = jnp.concatenate([block[0:ROWS] for block in blocks], axis=0)
        keys = jnp.concatenate([key4[images[0]], texts[0], key4[images[1]], texts[1]], axis=0)
        values = jnp.concatenate([val4[images[0]], texts[0], val4[images[1]], texts[1]], axis=0)
        length = jnp.where(first, lengths[0], lengths[1])
        visible = jnp.where(first, seen[0], seen[1])
        text_end = VIS + jnp.minimum(step_of + 1, length)
        allowed = (row < visible) | ((row >= VIS) & (row < text_end))
        scores = jnp.where(allowed, key_rows(dot(keys, queries, NT)) * SCALE, jnp.float32(-1e30))
        raw = jnp.exp(scores - jnp.max(scores, axis=0, keepdims=True))
        prob = raw * (1.0 / jnp.sum(raw, axis=0, keepdims=True))
        prob2 = diagonal([prob[0:VIS], none, prob[VIS:]])
        attended = dot(values, prob2, TN)
        live = (step_of < length).astype(jnp.float32)
        weighted = gain_t * attended * live
        loss_row = jnp.sum(weighted * attended, axis=0, keepdims=True) * (1.0 / (2.0 * TXT * HD))
        cot = weighted.astype(jnp.bfloat16)
        delta = jnp.sum(cot.astype(jnp.float32) * attended, axis=0, keepdims=True)
        prob_grad = value_rows(dot(values, cot, NN))
        score_grad2 = diagonal([prob * (prob_grad - delta), none])
        value_grad = dot(prob2, cot, NT)
        key_grad = dot(score_grad2, queries, NN) * SCALE
        zero = jnp.zeros_like(loss_row)
        losses = [jnp.where(first, loss_row, zero), jnp.where(first, zero, loss_row)]
        backs, visuals = [], []
        for i in range(2):
            base = i * KEYS
            backs.append(
                jnp.concatenate(
                    [key_grad[base + VIS : base + VIS + TXT], value_grad[base + VIS + TXT : base + KEYS]], axis=0
                ).astype(jnp.bfloat16)
            )
            visuals.append(
                jnp.concatenate([key_grad[base : base + VIS], value_grad[base : base + VIS]], axis=0)
                .astype(jnp.bfloat16)
                .astype(jnp.float32)
            )
        for image in range(4):
            acc[image] += jnp.where(images[0] == image, visuals[0], 0.0) + jnp.where(
                images[1] == image, visuals[1], 0.0
            )
        return backs, losses

    def back(slot, peer):
        pltpu.make_async_remote_copy(
            src_ref=back_send.at[slot],
            dst_ref=back_recv.at[slot],
            send_sem=back_send_sem.at[0],
            recv_sem=back_recv_sem.at[0],
            device_id=(peer, core),
            device_id_type=MESH,
        ).start()
        pltpu.make_async_remote_copy(
            src_ref=loss_send.at[pl.ds(slot, 1)],
            dst_ref=loss_recv.at[pl.ds(slot, 1)],
            send_sem=loss_send_sem.at[0],
            recv_sem=loss_recv_sem.at[0],
            device_id=(peer, core),
            device_id_type=MESH,
        ).start()

    def arrived(first_slot, count, chunk):
        pltpu.make_async_remote_copy(
            src_ref=send_buf.at[pl.ds(first_slot, count)],
            dst_ref=recv_buf.at[pl.ds(first_slot, count)],
            send_sem=send_sem.at[chunk],
            recv_sem=recv_sem.at[chunk],
            device_id=(me, core),
            device_id_type=MESH,
        ).wait_recv()

    def chunk_step(chunk, carry):
        arrived(chunk * CHUNK, CHUNK, chunk)
        for pair in range(CHUNK // 2):
            group, turn = 2 * chunk + pair // 2, 2 * (pair % 2)
            slot = 4 * group + turn
            peers = [origin(group, turn + i) for i in range(2)]
            backs, losses = work(slot, peers)
            for i in range(2):
                back_send[slot + i] = backs[i]
                loss_send[pl.ds(slot + i, 1)] = losses[i]
                back(slot + i, peers[i])
        return carry

    lax.fori_loop(0, 7, chunk_step, 0)
    arrived(56, 7, 7)
    for pair in range(CHUNK // 2):
        group, turn = 14 + pair // 2, 2 * (pair % 2)
        slot = 4 * group + turn
        peers = [origin(group, turn + i) for i in range(2)]
        backs, losses = work(slot, peers)
        for i in range(2):
            if slot + i < SLOTS - 1:
                back_send[slot + i] = backs[i]
                loss_send[pl.ds(slot + i, 1)] = losses[i]
                back(slot + i, peers[i])
            else:
                back_recv[slot + i] = backs[i]
                loss_recv[pl.ds(slot + i, 1)] = losses[i]

    for image in range(4):
        total = acc[image]
        vis_out[image] = jnp.concatenate([total[0:VIS], total[VIS : 2 * VIS]], axis=1).astype(jnp.bfloat16)

    remote = SLOTS - 1
    losses_in = pltpu.make_async_remote_copy(
        src_ref=loss_send.at[pl.ds(0, remote)],
        dst_ref=loss_recv.at[pl.ds(0, remote)],
        send_sem=loss_send_sem.at[0],
        recv_sem=loss_recv_sem.at[0],
        device_id=(me, core),
        device_id_type=MESH,
    )
    losses_in.wait_recv()
    per_slot = jnp.sum(loss_recv[...], axis=1, keepdims=True)
    slot_id = lax.broadcasted_iota(jnp.int32, (SLOTS, HD), 0)
    mine = jnp.sum(jnp.where(slot_id == place_ref[...], per_slot, 0.0), axis=0, keepdims=True)
    loss_parts[core] = mine
    for step in range(1, TENSOR):
        pltpu.make_async_remote_copy(
            src_ref=loss_parts.at[core],
            dst_ref=loss_parts.at[core],
            send_sem=part_send_sem.at[step],
            recv_sem=part_recv_sem.at[step],
            device_id=(me, (core + step) % TENSOR),
            device_id_type=MESH,
        ).start()

    backs_in = pltpu.make_async_remote_copy(
        src_ref=back_send.at[pl.ds(0, remote)],
        dst_ref=back_recv.at[pl.ds(0, remote)],
        send_sem=back_send_sem.at[0],
        recv_sem=back_recv_sem.at[0],
        device_id=(me, core),
        device_id_type=MESH,
    )
    backs_in.wait_recv()

    def place(response, carry):
        block = back_recv[meta[3, response]].astype(jnp.float32)
        text_out[response] = jnp.concatenate([block[0:TXT], block[TXT : 2 * TXT]], axis=1).astype(jnp.bfloat16)
        return carry

    lax.fori_loop(0, N_DP, place, 0, unroll=8)

    total = mine
    for step in range(1, TENSOR):
        peer = (core + TENSOR - step) % TENSOR
        pltpu.make_async_remote_copy(
            src_ref=loss_parts.at[peer],
            dst_ref=loss_parts.at[peer],
            send_sem=part_send_sem.at[step],
            recv_sem=part_recv_sem.at[step],
            device_id=(me, core),
            device_id_type=MESH,
        ).wait()
        total = total + loss_parts[peer]
    loss_out[...] = total

    losses_in.wait_send()
    backs_in.wait_send()
    for chunk in range(SLOTS // CHUNK):
        count = CHUNK if chunk < 7 else CHUNK - 1
        pltpu.make_async_remote_copy(
            src_ref=send_buf.at[pl.ds(chunk * CHUNK, count)],
            dst_ref=recv_buf.at[pl.ds(chunk * CHUNK, count)],
            send_sem=send_sem.at[chunk],
            recv_sem=recv_sem.at[chunk],
            device_id=(me, core),
            device_id_type=MESH,
        ).wait_send()


def local(queries, text_kv, visual_kv, loss_gain, response_image, visual_rows, text_length):
    me = lax.axis_index("dp")
    owned = visual_kv.shape[0]
    image_table = response_image.reshape(N_DP, N_DP)
    length_table = text_length.reshape(N_DP, N_DP)
    positions = jnp.arange(N_DP, dtype=jnp.int32)
    held = image_table // owned == me
    slot_image = jnp.sum(jnp.where(held, image_table % owned, 0), axis=1)
    slot_length = jnp.sum(jnp.where(held, length_table, 0), axis=1)
    owner = lax.dynamic_index_in_dim(image_table, me, 0, keepdims=False) // owned
    response_of = jnp.sum(jnp.where(owner[None, :] == positions[:, None], positions[None, :], 0), axis=1)
    dz = (owner // SIDE - me // SIDE + SIDE) % SIDE
    dy = (owner % SIDE - me % SIDE + SIDE) % SIDE
    slot_table = [0] * N_DP
    for group in range(16):
        for turn in range(4):
            a, b = offset(group, turn)
            slot_table[(a % SIDE) * SIDE + b % SIDE] = 4 * group + turn
    slot_of_offset = jnp.array(slot_table, dtype=jnp.int32)
    offset_id = dz * SIDE + dy
    place = jnp.sum(jnp.where(offset_id[:, None] == positions[None, :], slot_of_offset[None, :], 0), axis=1)
    meta = jnp.stack([response_of, slot_image, slot_length, place])
    rows4 = lax.dynamic_slice_in_dim(visual_rows, me * owned, owned)
    place_row = jnp.concatenate([place, jnp.full((HD - N_DP,), -1, jnp.int32)])[None, :]
    gain = loss_gain.reshape(HEADS, HD).T
    gain_t = jnp.tile(jnp.repeat(gain, TXT, axis=1), (1, 2))
    vmem = pl.BlockSpec(memory_space=pltpu.VMEM)
    smem = pl.BlockSpec(memory_space=pltpu.SMEM)
    vis_grad, text_grad, loss = pl.pallas_call(
        kernel,
        out_shape=(
            jax.ShapeDtypeStruct(visual_kv.shape, jnp.bfloat16),
            jax.ShapeDtypeStruct(text_kv.shape, jnp.bfloat16),
            jax.ShapeDtypeStruct((1, HD), jnp.float32),
        ),
        in_specs=[smem, smem] + [vmem] * 5,
        out_specs=[vmem] * 3,
        scratch_shapes=[
            pltpu.VMEM((SLOTS, BLOCK, HD), jnp.bfloat16),
            pltpu.VMEM((SLOTS, BLOCK, HD), jnp.bfloat16),
            pltpu.VMEM((4, VIS, HD), jnp.bfloat16),
            pltpu.VMEM((4, VIS, HD), jnp.bfloat16),
            pltpu.VMEM((4, 2 * VIS, HD), jnp.float32),
            pltpu.VMEM((SLOTS, 2 * TXT, HD), jnp.bfloat16),
            pltpu.VMEM((SLOTS, 2 * TXT, HD), jnp.bfloat16),
            pltpu.VMEM((SLOTS, HD), jnp.float32),
            pltpu.VMEM((SLOTS, HD), jnp.float32),
            pltpu.VMEM((TENSOR, 1, HD), jnp.float32),
            pltpu.SemaphoreType.DMA((8,)),
            pltpu.SemaphoreType.DMA((8,)),
            pltpu.SemaphoreType.DMA((1,)),
            pltpu.SemaphoreType.DMA((1,)),
            pltpu.SemaphoreType.DMA((1,)),
            pltpu.SemaphoreType.DMA((1,)),
            pltpu.SemaphoreType.DMA((TENSOR,)),
            pltpu.SemaphoreType.DMA((TENSOR,)),
        ],
        compiler_params=pltpu.CompilerParams(
            collective_id=0, has_side_effects=True, vmem_limit_bytes=32 * 1024 * 1024
        ),
        cost_estimate=pl.CostEstimate(flops=400_000_000, bytes_accessed=2_000_000, transcendentals=300_000),
    )(meta, rows4, queries, text_kv, visual_kv, gain_t, place_row)
    return vis_grad, text_grad, loss[0, :N_DP]


def solution(mesh):
    in_specs = (
        P("dp", None, "tensor"),
        P("dp", None, "tensor"),
        P("dp", None, "tensor"),
        P("tensor"),
        P(),
        P(),
        P(),
    )
    out_specs = (P("dp", None, "tensor"), P("dp", None, "tensor"), P("dp"))
    return jax.shard_map(local, mesh=mesh, in_specs=in_specs, out_specs=out_specs, check_vma=False)
```

time: 189 us -> 75.7 us (0.40)
  the two profiles are of different devices: /device:TPU:4 before, /device:TPU:1 now
where the time goes in v1:
time: 75.7 us; the launch traced here: 75.4 us
  Pallas kernels  68.1 us (90%)
  local copies, waits for them, and re-layouts  5.45 us (7%)
  other arithmetic  1.14 us (2%)
  between operations  0.77 us (1%)
    pallas_call x1, Pallas kernels, local(): pl.pallas_call(kernel, out_shape=(jax.ShapeDtypeStruct(visual_kv.shape, j...  68.1 us
    unnamed x12, local copies, waits for them, and re-layouts  3.19 us

profile of v1, /device:TPU:1, one launch (start us, length us, event | category | flops | bytes accessed | tf_op | source)
XLA Modules:
  0.0 75.4 jit_solution(9734372561688407131)
XLA Ops:
  0.6 0.0 copy-start
  0.6 0.0 copy-start.2
  0.7 0.8 %dynamic_slice.8.rows4 = s32[4]{0:T(128)S(1)} dynamic-slice(s32[256]{0:T(256)} %param.13, s32[]{:T(128)S(6)} %select_n.103), dynamic_slice_sizes={4} | dynamic-slice | bytes 36 | tf_op jit(solution)/shard_map/dynamic_slice | solution.py:335
  1.5 0.0 copy-done
  1.5 0.8 %reshape.102 = s32[64,64]{1,0:T(8,128)S(1)} reshape(s32[4096]{0:T(1024)} %param.12) | data formatting | bytes 32768 | tf_op jit(solution)/shard_map/reshape | solution.py:316
  2.3 0.8 %select_reduce_fusion = s32[64]{0:T(128)S(1)} fusion(s32[64]{0:T(128)} %constant.102.clone, s32[64]{0:T(128)S(1)} %fusion.5), kind=kLoop, calls=%fused_computation.8 | loop fusion | flops 12224 | bytes 768 | tf_op jit(solution)/shard_map/reduce_sum | solution.py:333
  3.2 0.1 select_reduce_fusion.2
  3.3 0.0 copy-start.4
  3.3 0.0 copy-start.3
  3.3 0.1 copy.11.gain_ref
  3.4 0.6 copy-done.4
  4.0 0.1 reshape.103
  4.1 0.1 fusion.2
  4.2 0.0 copy-done.2
  4.2 0.0 copy-done.3
  4.3 0.0 copy-start.1
  4.3 1.2 %copy-done.1 = bf16[64,8,1024]{2,1,0:T(8,128)(2,1)S(1)} copy-done((bf16[64,8,1024]{2,1,0:T(8,128)(2,1)S(1)}, bf16[64,8,1024]{2,1,0:T(8,128)(2,1)}, u32[]{:S(2)}) %copy-start.1) | copy-done | bytes 1048600
  5.5 68.1 %shard_map.103 = (bf16[4,64,256]{2,1,0:T(8,128)(2,1)S(1)}, bf16[64,8,256]{2,1,0:T(8,128)(2,1)S(1)}, f32[1,128]{1,0:T(1,128)S(1)}) custom-call(s32[4,64]{1,0:T(4,128)S(1)} %pad_add_fusion.meta, s32[4]{0:T(128)S(1)} %dynamic_slice.8.rows4, bf16[64,8,1024]{2,1,0:T(8,128)(2,1)S(1)} %copy-done.1, bf16[64,8,256]{2,1,0:T(8,128)(2,1)S(1)} %copy-done.2, ...), custom_call_target="tpu_custom_call" | custom-call | flops 400000000 | bytes 2000000 | tf_op jit(solution)/shard_map/pallas_call | solution.py:341
  73.6 0.5 slice_bitcast_fusion
  74.1 0.7 copy.14
  74.7 0.7 copy.15
  (6 shorter events, 0.1 us)
Async XLA Ops:
  0.6 0.8 %copy-start = (f32[1024]{0:T(1024)S(1)}, f32[1024]{0:T(1024)}, u32[]{:S(2)}) copy-start(f32[1024]{0:T(1024)} %param.11) | copy-start | bytes 12292
  0.6 3.6 %copy-start.2 = (bf16[64,8,256]{2,1,0:T(8,128)(2,1)S(1)}, bf16[64,8,256]{2,1,0:T(8,128)(2,1)}, u32[]{:S(2)}) copy-start(bf16[64,8,256]{2,1,0:T(8,128)(2,1)} %text_ref.1) | copy-start | bytes 786436
  3.3 0.7 copy-start.4
  3.3 0.9 %copy-start.3 = (bf16[4,64,256]{2,1,0:T(8,128)(2,1)S(1)}, bf16[4,64,256]{2,1,0:T(8,128)(2,1)}, u32[]{:S(2)}) copy-start(bf16[4,64,256]{2,1,0:T(8,128)(2,1)} %kv_ref.1) | copy-start | bytes 393220
  4.3 1.2 %copy-start.1 = (bf16[64,8,1024]{2,1,0:T(8,128)(2,1)S(1)}, bf16[64,8,1024]{2,1,0:T(8,128)(2,1)}, u32[]{:S(2)}) copy-start(bf16[64,8,1024]{2,1,0:T(8,128)(2,1)} %q_ref.1) | copy-start | bytes 3145732

commit v2 on v1

v2 whole, which is shorter than its diff:
```python
import functools

import jax
import jax.numpy as jnp
from jax import lax
from jax.experimental import pallas as pl
from jax.experimental.pallas import tpu as pltpu
from jax.sharding import PartitionSpec as P

HD = 128
MESH = pl.DeviceIdType.MESH
SIDE = 8
N_DP = 64
TENSOR = 8
VIS = 64
TXT = 8
HEADS = 8
ROWS = HEADS * TXT
BLOCK = ROWS + 2 * TXT
KEYS = VIS + 2 * TXT
CHUNK = 4
SLOTS = N_DP
SCALE = HD ** (-0.5)

NT = (((1,), (1,)), ((), ()))
NN = (((1,), (0,)), ((), ()))
TN = (((0,), (0,)), ((), ()))


def dot(left, right, dims):
    return lax.dot_general(left, right, dims, preferred_element_type=jnp.float32)


def offset(group, turn):
    traced = not isinstance(group, int)
    a, b = (1 + lax.rem(group, 4), 3 - lax.div(group, 4)) if traced else (1 + group % 4, 3 - group // 4)
    last = lax.div(group, 15) if traced else group // 15
    if turn == 0:
        return a, b
    if turn == 1:
        return b, -a
    if turn == 2:
        return -a, -b + 4 * last
    return -b, a - 4 * last


def kernel(
    queries, text_kv, visual_kv, gain, images, rows_of, lengths,
    vis_out, back_recv, loss_out, owner_out,
    q_ref, text_ref, kv_ref, gain_ref, image_ref, length_ref, rows, meta_vec, meta,
    send_buf, recv_buf, key4, val4, acc, back_send, loss_send, loss_recv, loss_parts,
    load_sem, send_sem, recv_sem, back_send_sem, back_recv_sem, loss_send_sem, loss_recv_sem, part_send_sem, part_recv_sem,
):
    me = lax.axis_index("dp")
    core = lax.axis_index("tensor")
    z, y = lax.div(me, SIDE), lax.rem(me, SIDE)

    ahead_z = [lax.rem(z + step, SIDE) for step in range(SIDE)]
    ahead_y = [lax.rem(y + step, SIDE) for step in range(SIDE)]

    def target(group, turn):
        dz, dy = offset(group, turn)
        return ahead_z[dz % SIDE] * SIDE + ahead_y[dy % SIDE]

    def origin(group, turn):
        dz, dy = offset(group, turn)
        return lax.rem(z - dz + SIDE, SIDE), lax.rem(y - dy + SIDE, SIDE)

    pairs = [
        (images, image_ref), (lengths, length_ref), (rows_of, rows), (queries, q_ref), (text_kv, text_ref),
        (visual_kv, kv_ref), (gain, gain_ref),
    ]
    loads = [pltpu.make_async_copy(src, dst, load_sem.at[n]) for n, (src, dst) in enumerate(pairs)]
    for load in loads:
        load.start()

    barrier = pltpu.get_barrier_semaphore()

    def greet(step, carry):
        peer = lax.rem(me + step, N_DP)
        pl.semaphore_signal(barrier, inc=1, device_id=(peer, core), device_id_type=MESH)
        return carry

    lax.fori_loop(1, N_DP, greet, 0)
    for step in range(1, TENSOR):
        pl.semaphore_signal(barrier, inc=1, device_id=(me, (core + step) % TENSOR), device_id_type=MESH)

    loads[0].wait()
    loads[1].wait()
    half = me % 2
    lane128 = lax.broadcasted_iota(jnp.int32, (HD, HD), 1)
    row128 = lax.broadcasted_iota(jnp.int32, (HD, HD), 0)
    owner_row = image_ref[pl.ds(me // 2, 1)] // 4
    own_lane = lane128 // N_DP == half
    chosen = (owner_row == row128) & own_lane
    index8 = (lax.broadcasted_iota(jnp.int32, (8, HD), 1) - N_DP * half).astype(jnp.float32).astype(jnp.bfloat16)
    response_of = dot(index8, chosen.astype(jnp.float32).astype(jnp.bfloat16), NT)
    image_table = image_ref[...]
    held = image_table // 4 == me
    local_image = image_table % 4
    code = jnp.where(held, local_image + 4 * length_ref[...], 0).astype(jnp.float32)
    loads[2].wait()
    first_row, first_col = lax.div(4 * me, HD), lax.rem(4 * me, HD)
    seen = jnp.zeros_like(image_table)
    for image in range(4):
        seen = jnp.where(local_image == image, rows[first_row, first_col + image], seen)
    seen = jnp.where(held, seen, 0).astype(jnp.float32)
    code = jnp.concatenate([code, seen, jnp.zeros((HD - 64, HD), jnp.float32)], axis=0).astype(jnp.bfloat16)
    part = lax.broadcasted_iota(jnp.int32, (8, HD), 1) // N_DP == lax.broadcasted_iota(jnp.int32, (8, HD), 0)
    codes = dot(part.astype(jnp.float32).astype(jnp.bfloat16), code, NT)
    meta_vec[0:8] = jnp.clip(response_of.astype(jnp.int32), 0, N_DP - 1)
    meta_vec[8:16] = jnp.clip(codes.astype(jnp.int32), 0, HD - 1)
    meta_vec[16:24] = jnp.broadcast_to(owner_row, (8, HD))
    owner_out[...] = jnp.where(half == 0, owner_row, pltpu.roll(owner_row, N_DP, 1))
    to_scalars = pltpu.make_async_copy(meta_vec, meta, load_sem.at[7])
    to_scalars.start()
    loads[3].wait()
    loads[4].wait()
    to_scalars.wait()

    def stage(slot, peer, where):
        response = jnp.clip(meta[0, peer], 0, N_DP - 1)
        wide = q_ref[response].astype(jnp.float32)
        stacked = jnp.concatenate([wide[:, h * HD : (h + 1) * HD] for h in range(HEADS)], axis=0)
        where[slot, 0:ROWS] = stacked.astype(jnp.bfloat16)
        text = text_ref[response].astype(jnp.float32)
        pair = jnp.concatenate([text[:, 0:HD], text[:, HD : 2 * HD]], axis=0)
        where[slot, ROWS:BLOCK] = pair.astype(jnp.bfloat16)

    def send(slot, peer):
        pltpu.make_async_remote_copy(
            src_ref=send_buf.at[slot],
            dst_ref=recv_buf.at[slot],
            send_sem=send_sem.at[slot // CHUNK],
            recv_sem=recv_sem.at[slot // CHUNK],
            device_id=(peer, core),
            device_id_type=MESH,
        ).start()

    pl.semaphore_wait(barrier, N_DP - 1 + TENSOR - 1)

    for group in range(15):
        for turn in range(4):
            slot, peer = 4 * group + turn, target(group, turn)
            stage(slot, peer, send_buf)
            send(slot, peer)
    for turn in range(3):
        stage(60 + turn, target(15, turn), send_buf)
        send(60 + turn, target(15, turn))
    stage(63, me, recv_buf)

    for load in loads[5:]:
        load.wait()
    for image in range(4):
        key4[image] = kv_ref[image, :, 0:HD]
        val4[image] = kv_ref[image, :, HD : 2 * HD]
    acc[...] = jnp.zeros_like(acc)
    per_row = jnp.concatenate([jnp.broadcast_to(gain_ref[h : h + 1], (TXT, HD)) for h in range(HEADS)] * 2, axis=0)
    gain_t = per_row.T

    lane = lax.broadcasted_iota(jnp.int32, (1, HD), 1)
    first = lane < ROWS
    step_of = lane % TXT
    row = lax.broadcasted_iota(jnp.int32, (VIS + TXT, HD), 0)

    def key_rows(both):
        return jnp.where(first, both[0 : VIS + TXT], both[KEYS : KEYS + VIS + TXT])

    def value_rows(both):
        both = [jnp.concatenate([both[b : b + VIS], both[b + VIS + TXT : b + KEYS]], axis=0) for b in (0, KEYS)]
        return jnp.where(first, both[0], both[1])

    none = jnp.zeros((TXT, HD), jnp.float32)

    def diagonal(parts):
        values = jnp.concatenate(parts, axis=0)
        zero = jnp.zeros_like(values)
        return jnp.concatenate([jnp.where(first, values, zero), jnp.where(first, zero, values)], axis=0).astype(
            jnp.bfloat16
        )

    def work(group):
        pairs = []
        for half_of in range(2):
            slot = 4 * group + 2 * half_of
            images, lengths, seen = [], [], []
            for i in range(2):
                from_z, from_y = origin(group, 2 * half_of + i)
                code_row, code_lane = 8 + lax.rem(from_y, 2), from_z * 4 + lax.div(from_y, 2)
                code = meta[code_row, code_lane]
                images.append(jnp.clip(lax.rem(code, 4), 0, 3))
                lengths.append(lax.div(code, 4))
                seen.append(meta[code_row, 32 + code_lane])
            blocks = [recv_buf[slot + i] for i in range(2)]
            texts = [block[ROWS:BLOCK] for block in blocks]
            queries = jnp.concatenate([block[0:ROWS] for block in blocks], axis=0)
            keys = jnp.concatenate([key4[images[0]], texts[0], key4[images[1]], texts[1]], axis=0)
            values = jnp.concatenate([val4[images[0]], texts[0], val4[images[1]], texts[1]], axis=0)
            length = jnp.where(first, lengths[0], lengths[1])
            visible = jnp.where(first, seen[0], seen[1])
            pairs.append((images, queries, keys, values, length, visible))
        scores = [dot(keys, queries, NT) for _, queries, keys, _, _, _ in pairs]
        probs = []
        for (_, _, _, _, length, visible), score in zip(pairs, scores):
            text_end = VIS + jnp.minimum(step_of + 1, length)
            allowed = (row < visible) | ((row >= VIS) & (row < text_end))
            score = jnp.where(allowed, key_rows(score) * SCALE, jnp.float32(-1e30))
            raw = jnp.exp(score - jnp.max(score, axis=0, keepdims=True))
            probs.append(raw * (1.0 / jnp.sum(raw, axis=0, keepdims=True)))
        probs2 = [diagonal([prob[0:VIS], none, prob[VIS:]]) for prob in probs]
        attended = [dot(pair[3], prob2, TN) for pair, prob2 in zip(pairs, probs2)]
        cots, deltas, losses = [], [], []
        for pair, out in zip(pairs, attended):
            live = (step_of < pair[4]).astype(jnp.float32)
            weighted = gain_t * out * live
            loss_row = jnp.sum(weighted * out, axis=0, keepdims=True) * (1.0 / (2.0 * TXT * HD))
            cot = weighted.astype(jnp.bfloat16)
            cots.append(cot)
            deltas.append(jnp.sum(cot.astype(jnp.float32) * out, axis=0, keepdims=True))
            zero = jnp.zeros_like(loss_row)
            losses += [jnp.where(first, loss_row, zero), jnp.where(first, zero, loss_row)]
        prob_grads = [dot(pair[3], cot, NN) for pair, cot in zip(pairs, cots)]
        value_grads = [dot(prob2, cot, NT) for prob2, cot in zip(probs2, cots)]
        key_grads = []
        for pair, prob, grad, delta in zip(pairs, probs, prob_grads, deltas):
            score_grad2 = diagonal([prob * (value_rows(grad) - delta), none])
            key_grads.append(dot(score_grad2, pair[1], NN) * SCALE)
        images, backs, visuals = [], [], []
        for pair, key_grad, value_grad in zip(pairs, key_grads, value_grads):
            images += pair[0]
            for base in (0, KEYS):
                text_grad = [key_grad[base + VIS : base + VIS + TXT], value_grad[base + VIS + TXT : base + KEYS]]
                backs.append(jnp.concatenate(text_grad, axis=0).astype(jnp.bfloat16))
                visual = [key_grad[base : base + VIS], value_grad[base : base + VIS]]
                visuals.append(jnp.concatenate(visual, axis=0).astype(jnp.bfloat16).astype(jnp.float32))
        for image in range(4):
            total = acc[image]
            for held_image, visual in zip(images, visuals):
                total = total + jnp.where(held_image == image, visual, 0.0)
            acc[image] = total
        return backs, losses

    def back(slot, peer):
        pltpu.make_async_remote_copy(
            src_ref=back_send.at[slot],
            dst_ref=back_recv.at[me],
            send_sem=back_send_sem.at[0],
            recv_sem=back_recv_sem.at[0],
            device_id=(peer, core),
            device_id_type=MESH,
        ).start()
        pltpu.make_async_remote_copy(
            src_ref=loss_send.at[pl.ds(slot, 1)],
            dst_ref=loss_recv.at[pl.ds(me, 1)],
            send_sem=loss_send_sem.at[0],
            recv_sem=loss_recv_sem.at[0],
            device_id=(peer, core),
            device_id_type=MESH,
        ).start()

    def arrived(first_slot, count, chunk):
        pltpu.make_async_remote_copy(
            src_ref=send_buf.at[pl.ds(first_slot, count)],
            dst_ref=recv_buf.at[pl.ds(first_slot, count)],
            send_sem=send_sem.at[chunk],
            recv_sem=recv_sem.at[chunk],
            device_id=(me, core),
            device_id_type=MESH,
        ).wait_recv()

    def group_step(group, carry):
        arrived(4 * group, CHUNK, group)
        backs, losses = work(group)
        for turn in range(4):
            back_send[4 * group + turn] = backs[turn]
            loss_send[pl.ds(4 * group + turn, 1)] = losses[turn]
        for turn in range(4):
            from_z, from_y = origin(group, turn)
            back(4 * group + turn, from_z * SIDE + from_y)
        return carry

    lax.fori_loop(0, 15, group_step, 0)
    arrived(60, 3, 15)
    backs, losses = work(15)
    for turn in range(3):
        back_send[60 + turn] = backs[turn]
        loss_send[pl.ds(60 + turn, 1)] = losses[turn]
    for turn in range(3):
        from_z, from_y = origin(15, turn)
        back(60 + turn, from_z * SIDE + from_y)
    back_recv[me] = backs[3]
    loss_recv[pl.ds(me, 1)] = losses[3]

    for image in range(4):
        total = acc[image]
        vis_out[image] = jnp.concatenate([total[0:VIS], total[VIS : 2 * VIS]], axis=1).astype(jnp.bfloat16)

    remote = SLOTS - 1
    losses_in = pltpu.make_async_remote_copy(
        src_ref=loss_send.at[pl.ds(0, remote)],
        dst_ref=loss_recv.at[pl.ds(0, remote)],
        send_sem=loss_send_sem.at[0],
        recv_sem=loss_recv_sem.at[0],
        device_id=(me, core),
        device_id_type=MESH,
    )
    losses_in.wait_recv()
    per_slot = jnp.sum(loss_recv[...], axis=1, keepdims=True)
    slot_id = lax.broadcasted_iota(jnp.int32, (SLOTS, HD), 0)
    mine = jnp.sum(jnp.where(slot_id == owner_row, per_slot, 0.0), axis=0, keepdims=True)
    loss_parts[core] = mine
    for step in range(1, TENSOR):
        pltpu.make_async_remote_copy(
            src_ref=loss_parts.at[core],
            dst_ref=loss_parts.at[core],
            send_sem=part_send_sem.at[step],
            recv_sem=part_recv_sem.at[step],
            device_id=(me, (core + step) % TENSOR),
            device_id_type=MESH,
        ).start()

    backs_in = pltpu.make_async_remote_copy(
        src_ref=back_send.at[pl.ds(0, remote)],
        dst_ref=back_recv.at[pl.ds(0, remote)],
        send_sem=back_send_sem.at[0],
        recv_sem=back_recv_sem.at[0],
        device_id=(me, core),
        device_id_type=MESH,
    )
    backs_in.wait_recv()

    total = mine
    for step in range(1, TENSOR):
        peer = (core + TENSOR - step) % TENSOR
        pltpu.make_async_remote_copy(
            src_ref=loss_parts.at[peer],
            dst_ref=loss_parts.at[peer],
            send_sem=part_send_sem.at[step],
            recv_sem=part_recv_sem.at[step],
            device_id=(me, core),
            device_id_type=MESH,
        ).wait()
        total = total + loss_parts[peer]
    loss_out[...] = jnp.where(half == 0, total, pltpu.roll(total, N_DP, 1))

    losses_in.wait_send()
    backs_in.wait_send()
    for chunk in range(SLOTS // CHUNK):
        count = CHUNK if chunk < 15 else CHUNK - 1
        pltpu.make_async_remote_copy(
            src_ref=send_buf.at[pl.ds(chunk * CHUNK, count)],
            dst_ref=recv_buf.at[pl.ds(chunk * CHUNK, count)],
            send_sem=send_sem.at[chunk],
            recv_sem=recv_sem.at[chunk],
            device_id=(me, core),
            device_id_type=MESH,
        ).wait_send()


def finish(owner, vis, back, loss, vis_out, text_out, loss_out):
    def place(response, carry):
        block = back[owner[0, response]].astype(jnp.float32)
        text_out[response] = jnp.concatenate([block[0:TXT], block[TXT : 2 * TXT]], axis=1).astype(jnp.bfloat16)
        return carry

    lax.fori_loop(0, N_DP, place, 0, unroll=8)
    vis_out[...] = vis[...]
    loss_out[...] = loss[0, 0:N_DP]


def local(queries, text_kv, visual_kv, loss_gain, response_image, visual_rows, text_length):
    vmem = pl.BlockSpec(memory_space=pltpu.VMEM)
    vis, back, loss, owner = pl.pallas_call(
        kernel,
        out_shape=(
            jax.ShapeDtypeStruct(visual_kv.shape, jnp.bfloat16),
            jax.ShapeDtypeStruct((SLOTS, 2 * TXT, HD), jnp.bfloat16),
            jax.ShapeDtypeStruct((1, HD), jnp.float32),
            jax.ShapeDtypeStruct((1, HD), jnp.int32),
        ),
        in_specs=[pl.BlockSpec(memory_space=pltpu.HBM)] * 7,
        out_specs=(vmem, vmem, vmem, vmem),
        scratch_shapes=[
            pltpu.VMEM(queries.shape, jnp.bfloat16),
            pltpu.VMEM(text_kv.shape, jnp.bfloat16),
            pltpu.VMEM(visual_kv.shape, jnp.bfloat16),
            pltpu.VMEM((HEADS, HD), jnp.float32),
            pltpu.VMEM((32, HD), jnp.int32),
            pltpu.VMEM((32, HD), jnp.int32),
            pltpu.SMEM((2, HD), jnp.int32),
            pltpu.VMEM((24, HD), jnp.int32),
            pltpu.SMEM((24, HD), jnp.int32),
            pltpu.VMEM((SLOTS, BLOCK, HD), jnp.bfloat16),
            pltpu.VMEM((SLOTS, BLOCK, HD), jnp.bfloat16),
            pltpu.VMEM((4, VIS, HD), jnp.bfloat16),
            pltpu.VMEM((4, VIS, HD), jnp.bfloat16),
            pltpu.VMEM((4, 2 * VIS, HD), jnp.float32),
            pltpu.VMEM((SLOTS, 2 * TXT, HD), jnp.bfloat16),
            pltpu.VMEM((SLOTS, HD), jnp.float32),
            pltpu.VMEM((SLOTS, HD), jnp.float32),
            pltpu.VMEM((TENSOR, 1, HD), jnp.float32),
            pltpu.SemaphoreType.DMA((8,)),
            pltpu.SemaphoreType.DMA((SLOTS // CHUNK,)),
            pltpu.SemaphoreType.DMA((SLOTS // CHUNK,)),
            pltpu.SemaphoreType.DMA((1,)),
            pltpu.SemaphoreType.DMA((1,)),
            pltpu.SemaphoreType.DMA((1,)),
            pltpu.SemaphoreType.DMA((1,)),
            pltpu.SemaphoreType.DMA((TENSOR,)),
            pltpu.SemaphoreType.DMA((TENSOR,)),
        ],
        compiler_params=pltpu.CompilerParams(
            collective_id=0, has_side_effects=True, vmem_limit_bytes=60 * 1024 * 1024
        ),
        cost_estimate=pl.CostEstimate(flops=400_000_000, bytes_accessed=2_000_000, transcendentals=300_000),
    )(
        queries,
        text_kv,
        visual_kv,
        loss_gain.reshape(HEADS, HD),
        response_image.reshape(32, HD),
        visual_rows.reshape(2, HD),
        text_length.reshape(32, HD),
    )
    return pl.pallas_call(
        finish,
        out_shape=(
            jax.ShapeDtypeStruct(visual_kv.shape, jnp.bfloat16),
            jax.ShapeDtypeStruct(text_kv.shape, jnp.bfloat16),
            jax.ShapeDtypeStruct((N_DP,), jnp.float32),
        ),
        in_specs=[pl.BlockSpec(memory_space=pltpu.SMEM), vmem, vmem, vmem],
        out_specs=(vmem, vmem, vmem),
    )(owner, vis, back, loss)


def solution(mesh):
    in_specs = (
        P("dp", None, "tensor"),
        P("dp", None, "tensor"),
        P("dp", None, "tensor"),
        P("tensor"),
        P(),
        P(),
        P(),
    )
    out_specs = (P("dp", None, "tensor"), P("dp", None, "tensor"), P("dp"))
    return jax.shard_map(local, mesh=mesh, in_specs=in_specs, out_specs=out_specs, check_vma=False)
```

time: 75.7 us -> 67.6 us (0.89)
  local copies, waits for them, and re-layouts: 5.45 us -> 0 us
  Pallas kernels: 68.1 us -> 66.8 us
  other arithmetic: 1.14 us -> 0 us
    unnamed x12 -> x0, local copies, waits for them, and re-layouts: 3.19 us -> none
    pallas_call x1, Pallas kernels: 68.1 us -> 64.9 us  [local(): pl.pallas_call(kernel, out_shape=(jax.ShapeDtypeStruct(visual_kv.shape, j...]
    pallas_call x0 -> x1, Pallas kernels: none -> 1.85 us  [local(): pl.pallas_call(finish, out_shape=(jax.ShapeDtypeStruct(visual_kv.shape, j...]
    reduce_sum x3 -> x0, other arithmetic: 1.07 us -> none  [the longest x1 0.83 us: local(): jnp.sum(jnp.where(offset_id[:, None] == positions[None, :], slot_of_offse...]
    reshape x2 -> x0, local copies, waits for them, and re-layouts: 0.86 us -> none  [the longest x1 0.79 us: local(): image_table = response_image.reshape(N_DP, N_DP)]
    dynamic_slice x1 -> x0, local copies, waits for them, and re-layouts: 0.79 us -> none  [local(): rows4 = lax.dynamic_slice_in_dim(visual_rows, me * owned, owned)]
where the time goes in v2:
time: 67.6 us; the launch traced here: 67.4 us
  Pallas kernels  66.8 us (99%)
    pallas_call x1, Pallas kernels, local(): pl.pallas_call(kernel, out_shape=(jax.ShapeDtypeStruct(visual_kv.shape, j...  64.9 us
    pallas_call x1, Pallas kernels, local(): pl.pallas_call(finish, out_shape=(jax.ShapeDtypeStruct(visual_kv.shape, j...  1.85 us

profile of v2, /device:TPU:1, one launch (start us, length us, event | category | flops | bytes accessed | tf_op | source)
XLA Modules:
  0.0 67.4 jit_solution(11575601485334977358)
XLA Ops:
  0.6 64.9 %shard_map.94 = (bf16[4,64,256]{2,1,0:T(8,128)(2,1)}, bf16[64,16,128]{2,1,0:T(8,128)(2,1)}, f32[1,128]{1,0:T(1,128)}, s32[1,128]{1,0:T(1,128)}) custom-call(bf16[64,8,1024]{2,1,0:T(8,128)(2,1)} %queries.1, bf16[64,8,256]{2,1,0:T(8,128)(2,1)} %text_kv.1, bf16[4,64,256]{2,1,0:T(8,128)(2,1)} %visual_kv.1, f32[8,128]{1,0:T(8,128)} %bitcast.6, ...), custom_call_target="tpu_custom_call" | custom-call | flops 400000000 | bytes 2000000 | tf_op jit(solution)/shard_map/pallas_call | solution.py:373
  65.6 1.8 %shard_map.95 = (bf16[4,64,256]{2,1,0:T(8,128)(2,1)}, bf16[64,8,256]{2,1,0:T(8,128)(2,1)}, f32[64]{0:T(128)}) custom-call(s32[1,128]{1,0:T(1,128)} %get-tuple-element.7.owner, bf16[4,64,256]{2,1,0:T(8,128)(2,1)} %get-tuple-element.8.vis, bf16[64,16,128]{2,1,0:T(8,128)(2,1)} %get-tuple-element.9.back, f32[1,128]{1,0:T(1,128)} %get-tuple-element.10.loss), custom_call_target="tpu_custom_call" | custom-call | tf_op jit(solution)/shard_map/pallas_call | solution.py:425

commit v3 on v2

--- a/solution.py
+++ b/solution.py
@@ -31,17 +31,15 @@
     return lax.dot_general(left, right, dims, preferred_element_type=jnp.float32)
 
 
+def turned(a, b):
+    return ((a, b), (-a, -b), (b, -a), (-b, a))
+
+
+TABLE = (((4, 4), (4, 0), (0, 4), (0, 0)),) + tuple(turned(*ab) for ab in ((4, 3), (1, 0), (3, 3), (2, 0), (4, 2), (1, 1), (2, 3), (3, 0), (3, 2), (2, 1), (4, 1), (1, 2), (1, 3), (3, 1), (2, 2)))
+
+
 def offset(group, turn):
-    traced = not isinstance(group, int)
-    a, b = (1 + lax.rem(group, 4), 3 - lax.div(group, 4)) if traced else (1 + group % 4, 3 - group // 4)
-    last = lax.div(group, 15) if traced else group // 15
-    if turn == 0:
-        return a, b
-    if turn == 1:
-        return b, -a
-    if turn == 2:
-        return -a, -b + 4 * last
-    return -b, a - 4 * last
+    return TABLE[group][turn]
 
 
 def kernel(
@@ -139,15 +137,13 @@
 
     pl.semaphore_wait(barrier, N_DP - 1 + TENSOR - 1)
 
-    for group in range(15):
-        for turn in range(4):
-            slot, peer = 4 * group + turn, target(group, turn)
+    for slot in range(SLOTS):
+        if slot == 3:
+            stage(slot, me, recv_buf)
+        else:
+            peer = target(slot // CHUNK, slot % CHUNK)
             stage(slot, peer, send_buf)
             send(slot, peer)
-    for turn in range(3):
-        stage(60 + turn, target(15, turn), send_buf)
-        send(60 + turn, target(15, turn))
-    stage(63, me, recv_buf)
 
     for load in loads[5:]:
         load.wait()
@@ -279,17 +275,20 @@
             back(4 * group + turn, from_z * SIDE + from_y)
         return carry
 
-    lax.fori_loop(0, 15, group_step, 0)
-    arrived(60, 3, 15)
-    backs, losses = work(15)
-    for turn in range(3):
-        back_send[60 + turn] = backs[turn]
-        loss_send[pl.ds(60 + turn, 1)] = losses[turn]
-    for turn in range(3):
-        from_z, from_y = origin(15, turn)
-        back(60 + turn, from_z * SIDE + from_y)
-    back_recv[me] = backs[3]
-    loss_recv[pl.ds(me, 1)] = losses[3]
+    for group in range(16):
+        if group != 0:
+            group_step(group, 0)
+            continue
+        arrived(4 * group, 3, group)
+        backs, losses = work(group)
+        for turn in range(3):
+            back_send[4 * group + turn] = backs[turn]
+            loss_send[pl.ds(4 * group + turn, 1)] = losses[turn]
+        for turn in range(3):
+            from_z, from_y = origin(group, turn)
+            back(4 * group + turn, from_z * SIDE + from_y)
+        back_recv[me] = backs[3]
+        loss_recv[pl.ds(me, 1)] = losses[3]
 
     for image in range(4):
         total = acc[image]
@@ -346,7 +345,7 @@
     losses_in.wait_send()
     backs_in.wait_send()
     for chunk in range(SLOTS // CHUNK):
-        count = CHUNK if chunk < 15 else CHUNK - 1
+        count = CHUNK if chunk != 0 else 3
         pltpu.make_async_remote_copy(
             src_ref=send_buf.at[pl.ds(chunk * CHUNK, count)],
             dst_ref=recv_buf.at[pl.ds(chunk * CHUNK, count)],

time: 67.6 us -> 63.7 us (0.942)
  Pallas kernels: 66.8 us -> 62.8 us
    pallas_call x1, Pallas kernels: 64.9 us -> 61 us  [local(): pl.pallas_call(kernel, out_shape=(jax.ShapeDtypeStruct(visual_kv.shape, j...]
where the time goes in v3:
time: 63.7 us; the launch traced here: 63.5 us
  Pallas kernels  62.8 us (99%)
  between operations  0.64 us (1%)
    pallas_call x1, Pallas kernels, local(): pl.pallas_call(kernel, out_shape=(jax.ShapeDtypeStruct(visual_kv.shape, j...  61 us
    pallas_call x1, Pallas kernels, local(): pl.pallas_call(finish, out_shape=(jax.ShapeDtypeStruct(visual_kv.shape, j...  1.85 us

profile of v3, /device:TPU:1, one launch (start us, length us, event | category | flops | bytes accessed | tf_op | source)
XLA Modules:
  0.0 63.5 jit_solution(4520904313911073369)
XLA Ops:
  0.6 61.0 %shard_map.94 = (bf16[4,64,256]{2,1,0:T(8,128)(2,1)}, bf16[64,16,128]{2,1,0:T(8,128)(2,1)}, f32[1,128]{1,0:T(1,128)}, s32[1,128]{1,0:T(1,128)}) custom-call(bf16[64,8,1024]{2,1,0:T(8,128)(2,1)} %queries.1, bf16[64,8,256]{2,1,0:T(8,128)(2,1)} %text_kv.1, bf16[4,64,256]{2,1,0:T(8,128)(2,1)} %visual_kv.1, f32[8,128]{1,0:T(8,128)} %bitcast.6, ...), custom_call_target="tpu_custom_call" | custom-call | flops 400000000 | bytes 2000000 | tf_op jit(solution)/shard_map/pallas_call | solution.py:372
  61.6 1.8 %shard_map.95 = (bf16[4,64,256]{2,1,0:T(8,128)(2,1)}, bf16[64,8,256]{2,1,0:T(8,128)(2,1)}, f32[64]{0:T(128)}) custom-call(s32[1,128]{1,0:T(1,128)} %get-tuple-element.7.owner, bf16[4,64,256]{2,1,0:T(8,128)(2,1)} %get-tuple-element.8.vis, bf16[64,16,128]{2,1,0:T(8,128)(2,1)} %get-tuple-element.9.back, f32[1,128]{1,0:T(1,128)} %get-tuple-element.10.loss), custom_call_target="tpu_custom_call" | custom-call | tf_op jit(solution)/shard_map/pallas_call | solution.py:424

commit v4 on v3

--- a/solution.py
+++ b/solution.py
@@ -20,6 +20,7 @@
 KEYS = VIS + 2 * TXT
 CHUNK = 4
 SLOTS = N_DP
+SELF = 3
 SCALE = HD ** (-0.5)
 
 NT = (((1,), (1,)), ((), ()))
@@ -245,6 +246,8 @@
             device_id=(peer, core),
             device_id_type=MESH,
         ).start()
+
+    def back_loss(slot, peer):
         pltpu.make_async_remote_copy(
             src_ref=loss_send.at[pl.ds(slot, 1)],
             dst_ref=loss_recv.at[pl.ds(me, 1)],
@@ -264,31 +267,26 @@
             device_id_type=MESH,
         ).wait_recv()
 
-    def group_step(group, carry):
-        arrived(4 * group, CHUNK, group)
+    def give_back(group):
+        for turn in range(CHUNK if group else SELF):
+            from_z, from_y = origin(group, turn)
+            back(4 * group + turn, from_z * SIDE + from_y)
+
+    for group in range(16):
+        count = CHUNK if group else SELF
+        arrived(4 * group, count, group)
         backs, losses = work(group)
-        for turn in range(4):
+        for turn in range(count):
             back_send[4 * group + turn] = backs[turn]
             loss_send[pl.ds(4 * group + turn, 1)] = losses[turn]
-        for turn in range(4):
+        if group == 0:
+            back_recv[me] = backs[SELF]
+            loss_recv[pl.ds(me, 1)] = losses[SELF]
+        for turn in range(count):
             from_z, from_y = origin(group, turn)
-            back(4 * group + turn, from_z * SIDE + from_y)
-        return carry
-
-    for group in range(16):
-        if group != 0:
-            group_step(group, 0)
-            continue
-        arrived(4 * group, 3, group)
-        backs, losses = work(group)
-        for turn in range(3):
-            back_send[4 * group + turn] = backs[turn]
-            loss_send[pl.ds(4 * group + turn, 1)] = losses[turn]
-        for turn in range(3):
-            from_z, from_y = origin(group, turn)
-            back(4 * group + turn, from_z * SIDE + from_y)
-        back_recv[me] = backs[3]
-        loss_recv[pl.ds(me, 1)] = losses[3]
+            back_loss(4 * group + turn, from_z * SIDE + from_y)
+    for group in sorted(range(16), key=lambda group: -sum(abs(step) for step in TABLE[group][0])):
+        give_back(group)
 
     for image in range(4):
         total = acc[image]

time: 63.7 us -> 62.6 us (0.983)
  Pallas kernels: 62.8 us -> 61.7 us
    pallas_call x1, Pallas kernels: 61 us -> 59.9 us  [local(): pl.pallas_call(kernel, out_shape=(jax.ShapeDtypeStruct(visual_kv.shape, j...]
where the time goes in v4:
time: 62.6 us; the launch traced here: 62.4 us
  Pallas kernels  61.7 us (99%)
  between operations  0.64 us (1%)
    pallas_call x1, Pallas kernels, local(): pl.pallas_call(kernel, out_shape=(jax.ShapeDtypeStruct(visual_kv.shape, j...  59.9 us
    pallas_call x1, Pallas kernels, local(): pl.pallas_call(finish, out_shape=(jax.ShapeDtypeStruct(visual_kv.shape, j...  1.85 us

profile of v4, /device:TPU:1, one launch (start us, length us, event | category | flops | bytes accessed | tf_op | source)
XLA Modules:
  0.0 62.4 jit_solution(17934196233372746410)
XLA Ops:
  0.6 59.9 %shard_map.94 = (bf16[4,64,256]{2,1,0:T(8,128)(2,1)}, bf16[64,16,128]{2,1,0:T(8,128)(2,1)}, f32[1,128]{1,0:T(1,128)}, s32[1,128]{1,0:T(1,128)}) custom-call(bf16[64,8,1024]{2,1,0:T(8,128)(2,1)} %queries.1, bf16[64,8,256]{2,1,0:T(8,128)(2,1)} %text_kv.1, bf16[4,64,256]{2,1,0:T(8,128)(2,1)} %visual_kv.1, f32[8,128]{1,0:T(8,128)} %bitcast.6, ...), custom_call_target="tpu_custom_call" | custom-call | flops 400000000 | bytes 2000000 | tf_op jit(solution)/shard_map/pallas_call | solution.py:370
  60.5 1.8 %shard_map.95 = (bf16[4,64,256]{2,1,0:T(8,128)(2,1)}, bf16[64,8,256]{2,1,0:T(8,128)(2,1)}, f32[64]{0:T(128)}) custom-call(s32[1,128]{1,0:T(1,128)} %get-tuple-element.7.owner, bf16[4,64,256]{2,1,0:T(8,128)(2,1)} %get-tuple-element.8.vis, bf16[64,16,128]{2,1,0:T(8,128)(2,1)} %get-tuple-element.9.back, f32[1,128]{1,0:T(1,128)} %get-tuple-element.10.loss), custom_call_target="tpu_custom_call" | custom-call | tf_op jit(solution)/shard_map/pallas_call | solution.py:422

commit v5 on v4

--- a/solution.py
+++ b/solution.py
@@ -36,7 +36,7 @@
     return ((a, b), (-a, -b), (b, -a), (-b, a))
 
 
-TABLE = (((4, 4), (4, 0), (0, 4), (0, 0)),) + tuple(turned(*ab) for ab in ((4, 3), (1, 0), (3, 3), (2, 0), (4, 2), (1, 1), (2, 3), (3, 0), (3, 2), (2, 1), (4, 1), (1, 2), (1, 3), (3, 1), (2, 2)))
+TABLE = (((4, 4), (4, 0), (0, 4), (0, 0)),) + tuple(turned(*ab) for ab in ((4, 3), (1, 0), (4, 2), (1, 1), (3, 3), (2, 0), (4, 1), (1, 2), (2, 3), (2, 1), (3, 2), (3, 0), (1, 3), (3, 1), (2, 2)))
 
 
 def offset(group, turn):

time: 62.6 us -> 62.8 us (level)
  no operation moved by 1% of the time
where the time goes in v5:
time: 62.8 us; the launch traced here: 62.6 us
  Pallas kernels  61.9 us (99%)
  between operations  0.64 us (1%)
    pallas_call x1, Pallas kernels, local(): pl.pallas_call(kernel, out_shape=(jax.ShapeDtypeStruct(visual_kv.shape, j...  60.1 us
    pallas_call x1, Pallas kernels, local(): pl.pallas_call(finish, out_shape=(jax.ShapeDtypeStruct(visual_kv.shape, j...  1.85 us

profile of v5, /device:TPU:1, one launch (start us, length us, event | category | flops | bytes accessed | tf_op | source)
XLA Modules:
  0.0 62.6 jit_solution(5354411078624815098)
XLA Ops:
  0.6 60.1 %shard_map.94 = (bf16[4,64,256]{2,1,0:T(8,128)(2,1)}, bf16[64,16,128]{2,1,0:T(8,128)(2,1)}, f32[1,128]{1,0:T(1,128)}, s32[1,128]{1,0:T(1,128)}) custom-call(bf16[64,8,1024]{2,1,0:T(8,128)(2,1)} %queries.1, bf16[64,8,256]{2,1,0:T(8,128)(2,1)} %text_kv.1, bf16[4,64,256]{2,1,0:T(8,128)(2,1)} %visual_kv.1, f32[8,128]{1,0:T(8,128)} %bitcast.6, ...), custom_call_target="tpu_custom_call" | custom-call | flops 400000000 | bytes 2000000 | tf_op jit(solution)/shard_map/pallas_call | solution.py:370
  60.7 1.8 %shard_map.95 = (bf16[4,64,256]{2,1,0:T(8,128)(2,1)}, bf16[64,8,256]{2,1,0:T(8,128)(2,1)}, f32[64]{0:T(128)}) custom-call(s32[1,128]{1,0:T(1,128)} %get-tuple-element.7.owner, bf16[4,64,256]{2,1,0:T(8,128)(2,1)} %get-tuple-element.8.vis, bf16[64,16,128]{2,1,0:T(8,128)(2,1)} %get-tuple-element.9.back, f32[1,128]{1,0:T(1,128)} %get-tuple-element.10.loss), custom_call_target="tpu_custom_call" | custom-call | tf_op jit(solution)/shard_map/pallas_call | solution.py:422
